TPU v7x, 32 devices: a whole 2x2x4 slice. The times are simulated.
32 devices in a mesh: section: 2 (over core), shard: 16 (over z, y, x).
Axes of the slice: x: 2, y: 2, z: 4, core: 2. Of those that a mesh axis runs over, the one named last changes fastest.
Arguments:
- hidden: bfloat16 [64, 32, 768], P('shard', None, 'section'), may hold values from -6 to 6
- proj: bfloat16 [768, 128], P('section'), may hold values from -0.21875 to 0.21875
- passages: bfloat16 [2048, 180, 128], P('shard'), may hold values from -24 to 24
- pass_len: int32 [2048], P('shard'), may hold values from 45 to 180
- query_len: int32 [64], P('shard'), may hold values from 8 to 32
- cand_owner: int32 [2, 64, 32, 1], P('section', 'shard'), may hold values from 0 to 15; in each aligned block of 128 rows (0 to 127, 128 to 255, ..., all dimensions but the last counted through in order) at most 16 rows name the same one
- cand_slot: int32 [2, 64, 32], P('section', 'shard'), may hold values from 0 to 127
- teacher: float32 [64, 64], P('shard', 'section'), may hold values from -18 to 318
Outputs:
- kl_div: float32 [64], P('shard')
- grad_hidden: bfloat16 [64, 32, 768], P('shard', None, 'section')
- grad_proj: float32 [768, 128], P('section')
Inputs may be any that keep to these rules, and one draw needn't show every extreme that they name: `cand_owner`: among the 128 candidates held by one device (one index of section, the queries of one index of shard), at most 16 name any one owner.
All inputs are finite; a program needn't handle non-finite values.
Results may differ from a plain program's by a relative error of at most 0.022.
Values may be sent and summed in bfloat16 or wider, within the bound.
A program may use at most 128 MiB of HBM per device.

v0:
```python
import jax
import jax.numpy as jnp
from jax import lax
from jax.sharding import PartitionSpec as P

SHARPNESS = 64.0
EPSILON = 1e-06
NEGATIVE = -1e30


def combined_all(value, axis, join):
    pieces = jax.tree.map(lambda part: lax.all_gather(part, axis), value)
    head = jax.tree.map(lambda part: part[0], pieces)
    tail = jax.tree.map(lambda part: part[1:], pieces)
    running, _ = lax.scan(lambda running, section: (join(running, section), None), head, tail)
    return running


def token_scores(q_rows, blocks, cand_lens):
    logits = (
        jnp.einsum("bid,btd->bit", q_rows, blocks, preferred_element_type=jnp.float32) * SHARPNESS
    )
    in_range = jnp.arange(blocks.shape[1])[None, None, :] < cand_lens[:, None, None]
    logits = jnp.where(in_range, logits, NEGATIVE)
    top_logit = jnp.max(logits, axis=2, keepdims=True)
    expo_terms = jnp.where(in_range, jnp.exp(logits - top_logit), 0.0)
    total = jnp.sum(expo_terms, axis=2, keepdims=True)
    token_max = (top_logit[..., 0] + jnp.log(total[..., 0])) / SHARPNESS
    return (token_max, expo_terms / total)


def merge_halves(first, second):
    teach_top = jnp.maximum(first[0], second[0])
    scale_one = jnp.exp(first[0] - teach_top)
    scale_two = jnp.exp(second[0] - teach_top)
    stud_top = jnp.maximum(first[3], second[3])
    fact_one = jnp.exp(first[3] - stud_top)
    fact_two = jnp.exp(second[3] - stud_top)
    return (
        teach_top,
        first[1] * scale_one + second[1] * scale_two,
        first[2] * scale_one + second[2] * scale_two,
        stud_top,
        first[4] * fact_one + second[4] * fact_two,
    )


def local(hidden, proj, passages, pass_len, query_len, cand_owner, cand_slot, teacher):
    num_queries, num_tokens, feat_half = hidden.shape
    vec_dim = proj.shape[1]
    pass_tokens = passages.shape[1]
    owners = lax.axis_size("shard")
    flat_h = hidden.reshape(num_queries * num_tokens, feat_half)
    partial_in = jnp.dot(flat_h, proj, preferred_element_type=jnp.float32).reshape(
        num_queries, num_tokens, vec_dim
    )
    proj_in = lax.psum(partial_in, "section")
    inv_norm = lax.rsqrt(jnp.sum(proj_in * proj_in, axis=2, keepdims=True) + EPSILON)
    query_vecs = (proj_in * inv_norm).astype(jnp.bfloat16)
    tok_mask = jnp.arange(num_tokens)[None, :] < query_len[:, None]
    owner_ids = cand_owner.reshape(-1)
    slot_ids = cand_slot.reshape(-1)
    requests = owner_ids.shape[0]
    cand_half = requests // num_queries
    capacity = max(2, (2 * requests + owners - 1) // owners)
    onehot = (owner_ids[:, None] == jnp.arange(owners)[None, :]).astype(jnp.int32)
    rank_ids = jnp.sum((jnp.cumsum(onehot, axis=0) - onehot) * onehot, axis=1)
    buf_pos = owner_ids * capacity + rank_ids
    query_of = jnp.arange(requests) // cand_half
    req_mask = tok_mask[query_of]
    slot_table = jnp.zeros((owners, capacity), jnp.int32).at[owner_ids, rank_ids].set(slot_ids)
    wanted = lax.all_to_all(slot_table, "shard", split_axis=0, concat_axis=0, tiled=True).reshape(
        -1
    )
    out_blocks = passages[wanted].reshape(owners, capacity, pass_tokens, vec_dim)
    out_lens = pass_len[wanted].reshape(owners, capacity)
    got_blocks, got_lens = (
        lax.all_to_all(out_blocks, "shard", split_axis=0, concat_axis=0, tiled=True),
        lax.all_to_all(out_lens, "shard", split_axis=0, concat_axis=0, tiled=True),
    )
    blocks = got_blocks.reshape(owners * capacity, pass_tokens, vec_dim)[buf_pos]
    cand_lens = got_lens.reshape(-1)[buf_pos]
    token_max, weight = token_scores(query_vecs[query_of], blocks, cand_lens)
    student = jnp.sum(jnp.where(req_mask, token_max, 0.0), axis=1).reshape(num_queries, cand_half)
    teach_top = jnp.max(teacher, axis=1)
    teach_exp = jnp.exp(teacher - teach_top[:, None])
    teach_sum = jnp.sum(teach_exp, axis=1)
    teach_wsum = jnp.sum(teach_exp * (teacher - student), axis=1)
    stud_top = jnp.max(student, axis=1)
    stud_sum = jnp.sum(jnp.exp(student - stud_top[:, None]), axis=1)
    top_teach, sum_teach, wsum_teach, top_stud, sum_stud = combined_all(
        (teach_top, teach_sum, teach_wsum, stud_top, stud_sum), "section", merge_halves
    )
    lse_teach = top_teach + jnp.log(sum_teach)
    lse_stud = top_stud + jnp.log(sum_stud)
    kl_div = wsum_teach / sum_teach - lse_teach + lse_stud
    score_grad = jnp.exp(student - lse_stud[:, None]) - jnp.exp(teacher - lse_teach[:, None])
    flat_grad = score_grad.reshape(-1)
    mixed = jnp.where(req_mask[:, :, None], flat_grad[:, None, None] * weight, 0.0).astype(
        jnp.bfloat16
    )
    part_grad = jnp.einsum("bit,btd->bid", mixed, blocks, preferred_element_type=jnp.float32)
    half_grad = jnp.sum(part_grad.reshape(num_queries, cand_half, num_tokens, vec_dim), axis=1)
    vec_grad = lax.psum(half_grad, "section")
    cubed = inv_norm * inv_norm * inv_norm
    in_grad = inv_norm * vec_grad - cubed * proj_in * jnp.sum(
        proj_in * vec_grad, axis=2, keepdims=True
    )
    flat_in = in_grad.astype(jnp.bfloat16).reshape(num_queries * num_tokens, vec_dim)
    grad_hidden = jnp.dot(flat_in, proj.T, preferred_element_type=jnp.float32).astype(jnp.bfloat16)
    grad_hidden = grad_hidden.reshape(num_queries, num_tokens, feat_half)
    local_proj = jnp.dot(flat_h.T, flat_in, preferred_element_type=jnp.float32)
    grad_proj = lax.psum(local_proj, "shard")
    return (kl_div, grad_hidden, grad_proj)


def solution(mesh):
    in_specs = (
        P("shard", None, "section"),
        P("section", None),
        P("shard", None, None),
        P("shard"),
        P("shard"),
        P("section", "shard", None, None),
        P("section", "shard", None),
        P("shard", "section"),
    )
    out_specs = (P("shard"), P("shard", None, "section"), P("section", None))
    return jax.shard_map(local, mesh=mesh, in_specs=in_specs, out_specs=out_specs, check_vma=False)
```

profile of v0, /device:TPU:0, one launch (start us, length us, event | category | flops | bytes accessed | tf_op | source)
XLA Modules:
  0.0 552.1 jit_solution(4688939597748267012)
XLA Ops:
  7.2 0.8 eq.15
  8.0 0.1 fusion.7
  8.1 0.2 reduce_window_sum.11
  8.2 0.2 select_reduce_fusion.1
  8.4 0.5 broadcast.235
  8.9 1.3 reduce.11
  10.3 0.1 reshape.292
  10.4 0.8 reshape.352
  11.2 7.0 %scatter_fusion = s32[16,16]{1,0:T(8,128)S(1)} fusion(s32[16,16]{1,0:T(8,128)S(1)} %broadcast_in_dim.30, s32[128]{0:T(128)S(1)} %get-tuple-element.59, s32[128]{0:T(128)S(1)} %reshape.352), kind=kCustom, calls=%fused_computation.6 | custom fusion | bytes 2560 | tf_op jit(solution)/shard_map/scatter | solution.py:71
  18.2 15.4 %all_to_all.23 = s32[16,1,16]{2,1,0:T(1,128)S(1)} all-to-all(s32[16,1,16]{2,1,0:T(1,128)S(1)} %bitcast.42), channel_id=1, replica_groups=mesh['section'=2,'shard'=16] {'shard'}, dimensions={0} | all-to-all | bytes 2048 | tf_op jit(solution)/shard_map/all_to_all | solution.py:72
  33.6 0.7 reduce.12
  34.2 0.1 reshape.294
  34.3 1.9 gather_fusion.1
  36.2 0.7 all_to_all.17
  36.9 3.5 all-to-all-start.1
  40.4 48.0 %gather_fusion.4 = bf16[256,180,128]{2,0,1:T(8,128)(2,1)} fusion(bf16[128,180,128]{2,0,1:T(8,128)(2,1)} %param.10, s32[1024]{0:T(1024)S(1)} %pad_clamp_fusion.1), kind=kCustom, calls=%fused_computation.4 | custom fusion | bytes 23593984 | tf_op jit(solution)/shard_map/gather | solution.py:75
  88.4 10.7 %copy.15 = bf16[16,16,180,128]{3,1,2,0:T(8,128)(2,1)} copy(bf16[16,16,180,128]{3,1,0,2:T(8,128)(2,1)} %bitcast.41) | data formatting | bytes 23592960 | tf_op jit(solution)/shard_map/reshape | solution.py:75
  99.1 6.9 %all-to-all-start.2 = ((bf16[16,16,180,128]{3,1,2,0:T(8,128)(2,1)}), bf16[16,16,180,128]{3,1,2,0:T(8,128)(2,1)}, u32[]{:S(2)}, u32[]{:S(2)}) async-start(bf16[16,16,180,128]{3,1,2,0:T(8,128)(2,1)} %copy.15), calls=%async_computation.2 | async-start | bytes 23592960 | tf_op jit(solution)/shard_map/all_to_all | solution.py:78
  105.9 0.0 all-reduce.10.cloned.1.call-start
  106.0 0.8 fusion.5
  106.8 0.0 all-reduce.10.cloned.1.call-update
  106.8 0.0 all-reduce.12.cloned.1.call-start
  106.9 0.1 iota_compare_fusion.2
  107.0 0.7 gather_fusion
  107.7 0.1 reduce_max.27
  107.8 0.6 dynamic-slice
  109.1 0.2 dynamic-update-slice.1
  109.3 0.7 reduce.13
  110.0 0.1 reshape.295
  110.1 1.3 gather_fusion.2
  111.4 0.1 iota_compare_fusion
  111.5 17.2 %all-reduce.10.cloned.1.call-done = f32[4,32,128]{2,1,0:T(8,128)} async-done(((f32[4,32,128]{2,1,0:T(8,128)}), f32[4,32,128]{2,1,0:T(8,128)}) %all-reduce.10.cloned.1.call-update) | async-done | bytes 65552 | tf_op jit(solution)/shard_map/psum | solution.py:57
  128.6 0.9 multiply_reduce_fusion.1
  129.6 0.9 multiply_convert_fusion
  130.5 0.8 gather_fusion.3
  131.3 189.5 %all-to-all-done.2 = bf16[16,16,180,128]{3,1,2,0:T(8,128)(2,1)} async-done(((bf16[16,16,180,128]{3,1,2,0:T(8,128)(2,1)}), bf16[16,16,180,128]{3,1,2,0:T(8,128)(2,1)}, u32[]{:S(2)}, u32[]{:S(2)}) %all-to-all-start.2) | async-done | bytes 11796512 | tf_op jit(solution)/shard_map/all_to_all | solution.py:78
  320.8 12.3 %copy.16 = bf16[16,16,180,128]{3,2,1,0:T(8,128)(2,1)} copy(bf16[16,16,180,128]{3,1,2,0:T(8,128)(2,1)} %all-to-all-done.2) | data formatting | bytes 23592960 | tf_op jit(solution)/shard_map/all_to_all | solution.py:78
  333.0 8.3 %gather_fusion.5 = bf16[128,180,128]{2,1,0:T(8,128)(2,1)} fusion(bf16[256,180,128]{2,1,0:T(8,128)(2,1)} %bitcast.43, s32[1024]{0:T(1024)S(1)} %pad_clamp_fusion), kind=kCustom, calls=%fused_computation.5 | custom fusion | bytes 11796992 | tf_op jit(solution)/shard_map/gather | solution.py:81
  341.4 6.6 %fusion = (f32[128,32]{1,0:T(8,128)S(1)}, f32[128,32,180]{2,1,0:T(8,128)S(1)}) fusion(pred[128,180]{1,0:T(8,128)(4,1)S(1)} %iota_compare_fusion, bf16[128,32,128]{2,1,0:T(8,128)(2,1)S(1)} %gather_fusion.3, bf16[128,180,128]{2,1,0:T(8,128)(2,1)} %gather_fusion.5), kind=kOutput, calls=%fused_computation.10 | convolution fusion | flops 190951424 | bytes 9935360 | tf_op jit(solution)/shard_map/bid,btd->bit/dot_general | solution.py:21
  348.0 1.9 copy-done.1
  349.9 1.8 fusion.1
  351.7 0.1 select_reduce_fusion
  351.9 0.1 reshape.298
  351.9 0.1 reduce_max.29
  352.1 0.2 multiply_reduce_fusion.2
  352.3 0.2 dynamic-update-slice.3
  352.5 0.2 dynamic-update-slice
  352.8 0.2 dynamic-update-slice.2
  353.0 0.2 dynamic-update-slice.4
  353.2 2.4 all-reduce.5
  355.6 0.6 subtract_add_fusion
  356.2 0.1 exponential_subtract_fusion
  356.3 0.1 mul.138
  356.4 6.0 %bitcast_reduce_fusion = f32[4,32,128]{2,1,0:T(8,128)} fusion(bf16[128,180,128]{2,1,0:T(8,128)(2,1)} %gather_fusion.5, f32[128,32,180]{2,1,0:T(8,128)} %copy-done.1, f32[128,32]{1,0:T(8,128)S(1)} %fusion.1, f32[128]{0:T(128)S(1)} %mul.138, f32[128,32]{1,0:T(8,128)S(1)} %get-tuple-element.60, pred[128,32]{1,0:T(8,128)(4,1)S(1)} %gather_fusion, ...), kind=kOutput, calls=%fused_computation.12 | convolution fusion | flops 195149824 | bytes 8973312 | tf_op jit(solution)/shard_map/bit,btd->bid/dot_general | solution.py:102
  362.4 0.0 all-reduce.12.cloned.1.call-update
  362.4 0.0 all-reduce.14.cloned.1.call-start
  362.4 67.5 %all-reduce.12.cloned.1.call-done = f32[4,32,128]{2,1,0:T(8,128)} async-done(((f32[4,32,128]{2,1,0:T(8,128)}), f32[4,32,128]{2,1,0:T(8,128)}) %all-reduce.12.cloned.1.call-update) | async-done | bytes 65552 | tf_op jit(solution)/shard_map/psum | solution.py:104
  429.9 0.9 multiply_reduce_fusion
  430.9 1.0 subtract_convert_fusion
  431.8 0.9 convolution_bitcast_fusion
  432.7 0.0 all-reduce.14.cloned.1.call-update
  432.8 0.8 convolution_convert_fusion
  433.6 110.2 %all-reduce.14.cloned.1.call-done = f32[384,128]{0,1:T(8,128)} async-done(((f32[384,128]{0,1:T(8,128)}), f32[384,128]{0,1:T(8,128)}) %all-reduce.14.cloned.1.call-update) | async-done | bytes 196624 | tf_op jit(solution)/shard_map/psum | solution.py:113
  543.8 1.7 copy.17
  (27 shorter events, 0.1 us)
Async XLA Ops:
  7.2 98.8 %copy-start = (bf16[4,32,384]{2,1,0:T(8,128)(2,1)S(1)}, bf16[4,32,384]{2,1,0:T(8,128)(2,1)}, u32[]{:S(2)}) copy-start(bf16[4,32,384]{2,1,0:T(8,128)(2,1)} %param.8) | copy-start | bytes 294916
  36.9 62.1 %all-to-all-start.1 = ((s32[16,1,16]{2,1,0:T(1,128)}), s32[16,1,16]{2,1,0:T(1,128)S(1)}, u32[]{:S(2)}, u32[]{:S(2)}) async-start(s32[16,1,16]{2,1,0:T(1,128)} %all_to_all.17), calls=%async_computation.1 | async-start | bytes 16384 | tf_op jit(solution)/shard_map/all_to_all | solution.py:79
  99.1 6.9 %copy-start.3 = (bf16[384,128]{1,0:T(8,128)(2,1)S(1)}, bf16[384,128]{1,0:T(8,128)(2,1)}, u32[]{:S(2)}) copy-start(bf16[384,128]{1,0:T(8,128)(2,1)} %param.9) | copy-start | bytes 294916
  99.1 7.9 %copy-start.5 = (s32[4]{0:T(128)S(1)}, s32[4]{0:T(128)}, u32[]{:S(2)}) copy-start(s32[4]{0:T(128)} %param.12) | copy-start | bytes 52
  99.1 8.6 %copy-start.4 = (f32[4,32]{1,0:T(4,128)S(1)}, f32[4,32]{1,0:T(4,128)}, u32[]{:S(2)}) copy-start(f32[4,32]{1,0:T(4,128)} %param.15) | copy-start | bytes 1540
  99.1 8.8 %copy-start.6 = (u32[32]{0:T(128)S(1)}, u32[32]{0:T(128)}, u32[]{:S(2)}) copy-start(u32[32]{0:T(128)} %constant.80) | copy-start | bytes 388
  99.1 221.7 %all-to-all-start.2 = ((bf16[16,16,180,128]{3,1,2,0:T(8,128)(2,1)}), bf16[16,16,180,128]{3,1,2,0:T(8,128)(2,1)}, u32[]{:S(2)}, u32[]{:S(2)}) async-start(bf16[16,16,180,128]{3,1,2,0:T(8,128)(2,1)} %copy.15), calls=%async_computation.2 | async-start | bytes 23592960 | tf_op jit(solution)/shard_map/all_to_all | solution.py:78
  105.9 22.7 %all-reduce.10.cloned.1.call-start = ((), (), s32[]{:S(2)}) async-start(), calls=%async_computation.3 | async-start | bytes 131072 | tf_op jit(solution)/shard_map/psum | solution.py:57
  106.8 323.1 %all-reduce.12.cloned.1.call-start = ((), (), s32[]{:S(2)}) async-start(), calls=%async_computation.4 | async-start | bytes 131072 | tf_op jit(solution)/shard_map/psum | solution.py:104
  348.0 1.9 copy-start.1
  356.4 73.6 %copy-start.2 = (f32[4,32,128]{2,1,0:T(8,128)S(1)}, f32[4,32,128]{2,1,0:T(8,128)}, u32[]{:S(2)}) copy-start(f32[4,32,128]{2,1,0:T(8,128)} %all-reduce.10.cloned.1.call-done) | copy-start | bytes 196612
  362.4 181.4 %all-reduce.14.cloned.1.call-start = ((), (), s32[]{:S(2)}) async-start(), calls=%async_computation.5 | async-start | bytes 393216 | tf_op jit(solution)/shard_map/psum | solution.py:113
Sparse Core Ops, SparseCore 0:
  109.6 18.9 all-reduce.9
  362.5 67.3 all-reduce.11
  435.8 107.9 all-reduce.13
where the time goes:
time: 553 us; the launch traced here: 552 us
  waiting for transfers between devices  384 us (69%)
  local copies, waits for them, and re-layouts  99.4 us (18%)
  blocking collectives  17.8 us (3%)
  matrix products  15.1 us (3%)
  between operations  14.6 us (3%)
  starting transfers between devices  10.4 us (2%)
  other arithmetic  10.1 us (2%)
    all_to_all x1, waiting for transfers between devices, local(): lax.all_to_all(out_blocks, 'shard', split_axis=0, concat_axis=0, tiled=True)  189 us
    psum x1, waiting for transfers between devices, local(): grad_proj = lax.psum(local_proj, 'shard')  110 us
    psum x1, waiting for transfers between devices, local(): vec_grad = lax.psum(half_grad, 'section')  67.5 us
    gather x1, local copies, waits for them, and re-layouts, local(): passages[wanted].reshape(owners, capacity, pass_tokens, vec_dim)  48 us
    psum x1, waiting for transfers between devices, local(): proj_in = lax.psum(partial_in, 'section')  17.2 us
    all_to_all x1, blocking collectives, local(): lax.all_to_all(slot_table, 'shard', split_axis=0, concat_axis=0, tiled=True)  15.4 us
    all_to_all x1, local copies, waits for them, and re-layouts, local(): lax.all_to_all(out_blocks, 'shard', split_axis=0, concat_axis=0, tiled=True)  12.3 us
  transfers between devices with their start and end apart: 5, of which 4 were waited for; matrix products, arithmetic and copies ran while one was open for 12% of the time, Pallas kernels for 0%

commit v1 on v0

v1 whole, which is shorter than its diff:
```python
import functools
import math

import jax
import jax.numpy as jnp
from jax import lax
from jax.experimental import pallas as pl
from jax.experimental.pallas import tpu as pltpu
from jax.sharding import PartitionSpec as P

SHARPNESS = 64.0
EPSILON = 1e-06
NEGATIVE = -1e30
LANES = 128
GROUP = 4
F32 = jnp.float32
BF16 = jnp.bfloat16
MESH = pl.DeviceIdType.MESH


def iota(shape, axis):
    return lax.broadcasted_iota(jnp.int32, shape, axis)


def remote(src, dst, send, recv, **where):
    return pltpu.make_async_remote_copy(
        src_ref=src, dst_ref=dst, send_sem=send, recv_sem=recv, device_id=where, device_id_type=MESH
    )


def enter(n, me, sec):
    barrier = pltpu.get_barrier_semaphore()
    pl.semaphore_signal(barrier, inc=1, device_id={"section": 1 - sec}, device_id_type=MESH)

    def greet(i, carry):
        pl.semaphore_signal(
            barrier, inc=1, device_id={"shard": lax.rem(me + i, n)}, device_id_type=MESH
        )
        return carry

    lax.fori_loop(1, n, greet, 0)
    pl.semaphore_wait(barrier, n)


def each_peer(n, me, body):
    def step(i, carry):
        body(lax.rem(me + i, n), i)
        return carry

    lax.fori_loop(1, n, step, 0)


def request_kernel(
    n, half_q, nt, h_ref, p_ref, meta_ref,
    q_out, pin_out, tab_out, code_out, info_out,
    part, opart, ometa, tab,
    sib_send, sib_recv, st, rt, sq, rq,
):
    sec, me = lax.axis_index("section"), lax.axis_index("shard")
    rows = half_q * nt
    enter(n, me, sec)
    meta_copy = remote(meta_ref, ometa, sib_send.at[0], sib_recv.at[0], section=1 - sec)
    meta_copy.start()
    part[...] = jnp.dot(h_ref[...], p_ref[...], preferred_element_type=F32)
    other_rows = pl.ds(pl.multiple_of((1 - sec) * rows, rows), rows)
    part_copy = remote(part.at[other_rows], opart, sib_send.at[1], sib_recv.at[1], section=1 - sec)
    part_copy.start()
    meta_copy.wait()

    width = meta_ref.shape[1]
    meta = jnp.concatenate([meta_ref[...], ometa[...]], axis=1)
    owner = meta[0:1, :].astype(jnp.int32)
    code, teach = meta[1:2, :], meta[2:3, :]
    query = meta[3:4, :].astype(jnp.int32)
    valid = (query >= sec * half_q) & (query < (sec + 1) * half_q)
    prob = jnp.zeros_like(teach)
    lane = iota((8, LANES), 1)
    info = jnp.zeros((8, LANES), F32)
    for j in range(half_q):
        mask = query == sec * half_q + j
        top = jnp.max(jnp.where(mask, teach, NEGATIVE), axis=1, keepdims=True)
        terms = jnp.where(mask, jnp.exp(jnp.where(mask, teach - top, 0.0)), 0.0)
        total = jnp.sum(terms, axis=1, keepdims=True)
        prob = prob + terms / total
        info = jnp.where(lane == j, top + jnp.log(total), info)
    info_out[...] = info
    named = jnp.where((iota((n, 2 * width), 0) == owner) & valid, 1.0, 0.0)
    before = jnp.where(iota((2 * width, 2 * width), 0) < iota((2 * width, 2 * width), 1), 1.0, 0.0)
    counts = jnp.dot(named.astype(BF16), before.astype(BF16), preferred_element_type=F32)
    rank = jnp.sum(named * counts, axis=0, keepdims=True).astype(jnp.int32)
    at_rank = jnp.where((iota((LANES, 2 * width), 0) == rank) & valid, 1.0, 0.0)
    line = iota((n * 8, 2 * width), 0)
    kind = line & 7
    value = jnp.where(kind == 0, code, jnp.where(kind == 1, prob, jnp.where(kind == 2, teach, 1.0)))
    value = jnp.where((lax.shift_right_logical(line, 3) == owner) & valid & (kind < 4), value, 0.0)
    table = lax.dot_general(
        value, at_rank, (((1,), (1,)), ((), ())),
        precision=lax.Precision.HIGHEST, preferred_element_type=F32,
    )
    tab[...] = table.reshape(n, 8, LANES)
    each_peer(n, me, lambda p, i: remote(
        tab.at[p], tab_out.at[me], st.at[i], rt.at[me], shard=p).start())
    tab_out[me] = tab[me]

    part_copy.wait()
    pin = part[pl.ds(pl.multiple_of(sec * rows, rows), rows), :] + opart[...]
    pin_out[...] = pin
    inv = lax.rsqrt(jnp.sum(pin * pin, axis=1, keepdims=True) + EPSILON)
    q_out[me] = (pin * inv).astype(BF16)
    each_peer(n, me, lambda p, i: remote(
        q_out.at[me], q_out.at[me], sq.at[i], rq.at[me], shard=p).start())
    each_peer(n, me, lambda p, i: remote(
        tab.at[p], tab_out.at[p], st.at[i], rt.at[p], shard=p).wait())
    got = tab_out[...]
    count = jnp.sum(got[:, 3, :], axis=1, keepdims=True)
    codes = jnp.where(iota((n, LANES), 1) == LANES - 1, count, got[:, 0, :])
    code_out[...] = (codes + 0.5).astype(jnp.int32)
    each_peer(n, me, lambda p, i: remote(
        q_out.at[me], q_out.at[p], sq.at[i], rq.at[p], shard=p).wait())


def score_kernel(
    n, half_q, nt, slot_bits, query_bits, cap,
    code, plen, q_ref, tab_ref, pas_hbm, a_out, t_out, stat_out,
    pas, u_ref, stud_ref, coef_ref, sem,
):
    load = pltpu.make_async_copy(pas_hbm, pas, sem)
    load.start()
    pass_tokens = pas.shape[1]
    scale = SHARPNESS * math.log2(math.e)
    stat_out[...] = jnp.where(iota(stat_out.shape, 0) == 0, NEGATIVE, 0.0)
    load.wait()
    tok = iota((nt, pass_tokens), 1)
    tok_row = iota((nt, 1), 0)

    def per_source(q, carry):
        cnt = code[q, LANES - 1]
        groups = lax.div(cnt + (GROUP - 1), GROUP)

        def group(g, carry):
            for k in range(GROUP):
                r = g * GROUP + k
                c = code[q, r]
                slot = jnp.maximum((c & ((1 << slot_bits) - 1)) - 1, 0)
                which = lax.shift_right_logical(c, slot_bits) & ((1 << query_bits) - 1)
                qlen = lax.shift_right_logical(c, slot_bits + query_bits)
                block = pas[slot]
                vecs = q_ref[q, pl.ds(pl.multiple_of(which * nt, nt), nt), :]
                logits = lax.dot_general(
                    vecs, block, (((1,), (1,)), ((), ())), preferred_element_type=F32
                )
                logits = jnp.where(tok < plen[slot], logits * scale, NEGATIVE)
                top = jnp.max(logits, axis=1, keepdims=True)
                terms = jnp.exp2(logits - top)
                total = jnp.sum(terms, axis=1, keepdims=True)
                best = top * (math.log(2.0) / SHARPNESS) + jnp.log(total) * (1.0 / SHARPNESS)
                student = jnp.sum(jnp.where(tok_row < qlen, best, 0.0), axis=0, keepdims=True)
                unit = jnp.dot(terms.astype(BF16), block, preferred_element_type=F32)
                u_ref[r] = unit * (1.0 / total)
                stud_ref[pl.ds(r, 1), :] = jnp.broadcast_to(student, (1, LANES))
            return carry

        lax.fori_loop(0, groups, group, 0)
        stud = stud_ref[...]
        row_id, lane_id = iota((cap, LANES), 0), iota((cap, LANES), 1)
        table = tab_ref[q]

        def column(v):
            return jnp.sum(
                jnp.where(row_id == lane_id, table[v : v + 1, :], 0.0), axis=1, keepdims=True
            )

        codes = (column(0) + 0.5).astype(jnp.int32)
        prob, teach = column(1), column(2)
        which = lax.shift_right_logical(codes, slot_bits) & ((1 << query_bits) - 1)
        stat = stat_out[...]
        stat_row, stat_lane = iota(stat.shape, 0), iota(stat.shape, 1)
        for j in range(half_q):
            mask = (row_id < cnt) & (which == j)
            top = jnp.max(jnp.where(mask, stud, NEGATIVE), axis=0, keepdims=True)
            terms = jnp.where(mask, jnp.exp(jnp.where(mask, stud - top, 0.0)), 0.0)
            total = jnp.sum(terms, axis=0, keepdims=True)
            cross = jnp.sum(jnp.where(mask, prob * (teach - stud), 0.0), axis=0, keepdims=True)
            coef_ref[j] = terms
            coef_ref[half_q + j] = jnp.where(mask, jnp.broadcast_to(prob, (cap, LANES)), 0.0)
            new = jnp.where(
                stat_row == 0, top[:, :1], jnp.where(stat_row == 1, total[:, :1], cross[:, :1])
            )
            stat = jnp.where((stat_lane == q * half_q + j) & (stat_row < 3), new, stat)
        stat_out[...] = stat

        def gather(g, sums):
            for k in range(GROUP):
                r = g * GROUP + k
                unit = u_ref[r]
                sums = tuple(
                    one + coef_ref[at, pl.ds(r, 1), :] * unit for at, one in enumerate(sums)
                )
            return sums

        zero = jnp.zeros(u_ref.shape[1:], F32)
        sums = lax.fori_loop(0, groups, gather, (zero,) * (2 * half_q))
        for j in range(half_q):
            a_out[q * half_q + j] = sums[j]
            t_out[q * half_q + j] = sums[half_q + j]
        return carry

    lax.fori_loop(0, n, per_source, 0)


def grad_kernel(
    n, half_q, nt, inside, qlen, a_ref, t_ref, stat_ref, pin_ref, info_ref, h_ref, p_ref,
    kl_out, gh_out, gp_out,
    stats, crow, psend, rpart, ing, klbuf, lp, rs,
    sib_send, sib_recv, s0, r0, s1, r1, s2, r2, s3, r3,
):
    sec, me = lax.axis_index("section"), lax.axis_index("shard")
    rows = half_q * nt
    width = stat_ref.shape[1]
    enter(n, me, sec)
    each_peer(n, me, lambda p, i: remote(
        stat_ref, stats.at[me], s0.at[i], r0.at[me], shard=p).start())
    stats[me] = stat_ref[...]
    each_peer(n, me, lambda p, i: remote(
        stat_ref, stats.at[p], s0.at[i], r0.at[p], shard=p).wait())
    tops, totals, crosses = stats[:, 0, :], stats[:, 1, :], stats[:, 2, :]
    top = jnp.max(tops, axis=0, keepdims=True)
    lse = top + jnp.log(jnp.sum(totals * jnp.exp(tops - top), axis=0, keepdims=True))
    cross = jnp.sum(crosses, axis=0, keepdims=True)
    factor = jnp.exp(stat_ref[0:1, :] - lse)
    count = crow.shape[0]
    crow[...] = jnp.broadcast_to(
        jnp.sum(
            jnp.where(iota((count, width), 0) == iota((count, width), 1), factor, 0.0),
            axis=1, keepdims=True,
        ),
        crow.shape,
    )

    def make_part(p):
        for j in range(half_q):
            at = p * half_q + j
            value = a_ref[at] * crow[pl.ds(at, 1), :] - t_ref[at]
            psend[p, j * nt : (j + 1) * nt, :] = value.astype(BF16)

    def send_part(p, i):
        make_part(p)
        remote(psend.at[p], rpart.at[me], s1.at[i], r1.at[me], shard=p).start()

    each_peer(n, me, send_part)
    make_part(me)
    rpart[me] = psend[me]

    kl = jnp.zeros((8, LANES), F32)
    lane = iota((1, width), 1)
    for j in range(half_q):
        mine = jnp.sum(jnp.where(lane == me * half_q + j, cross + lse, 0.0), axis=1, keepdims=True)
        kl = jnp.where(
            iota((8, LANES), 1) == sec * half_q + j, mine - info_ref[0:1, j : j + 1], kl
        )
    klbuf[sec] = kl
    kl_copy = remote(klbuf.at[sec], klbuf.at[sec], sib_send.at[0], sib_recv.at[0], section=1 - sec)
    kl_copy.start()
    pin = pin_ref[...]
    inv = lax.rsqrt(jnp.sum(pin * pin, axis=1, keepdims=True) + EPSILON)

    each_peer(n, me, lambda p, i: remote(
        psend.at[p], rpart.at[p], s1.at[i], r1.at[p], shard=p).wait())
    vec = lax.fori_loop(
        0, n, lambda o, total: total + rpart[o].astype(F32), jnp.zeros((rows, LANES), F32)
    )
    tok = iota((nt, LANES), 0)
    vec = jnp.concatenate(
        [
            jnp.where(tok < qlen[sec * half_q + j], vec[j * nt : (j + 1) * nt, :], 0.0)
            for j in range(half_q)
        ],
        axis=0,
    )
    grad = inv * vec - inv * inv * inv * pin * jnp.sum(pin * vec, axis=1, keepdims=True)
    own = pl.ds(pl.multiple_of(sec * rows, rows), rows)
    ing[own, :] = grad.astype(BF16)
    in_copy = remote(ing.at[own], ing.at[own], sib_send.at[1], sib_recv.at[1], section=1 - sec)
    in_copy.start()
    kl_copy.wait()
    kl_out[...] = klbuf[0] + klbuf[1]
    in_copy.wait()
    flat = ing[...]
    terms = lax.dot_general(
        h_ref[...], flat, (((0,), (0,)), ((), ())), preferred_element_type=F32
    )
    if inside:
        lp[...] = terms
        piece = terms.shape[0] // n

        def span(p):
            return pl.ds(pl.multiple_of(p * piece, 8), piece)

        each_peer(n, me, lambda p, i: remote(
            lp.at[span(p)], rs.at[me], s2.at[i], r2.at[me], shard=p).start())
        rs[me] = lp[span(me), :]
    else:
        gp_out[...] = terms
    gh_out[...] = lax.dot_general(
        flat, p_ref[...], (((1,), (1,)), ((), ())), preferred_element_type=F32
    ).astype(BF16)
    if inside:
        each_peer(n, me, lambda p, i: remote(
            lp.at[span(p)], rs.at[p], s2.at[i], r2.at[p], shard=p).wait())
        gp_out[span(me), :] = jnp.sum(rs[...], axis=0)
        each_peer(n, me, lambda p, i: remote(
            gp_out.at[span(me)], gp_out.at[span(me)], s3.at[i], r3.at[me], shard=p).start())
        each_peer(n, me, lambda p, i: remote(
            gp_out.at[span(me)], gp_out.at[span(p)], s3.at[i], r3.at[p], shard=p).wait())


def local(hidden, proj, passages, pass_len, query_len, cand_owner, cand_slot, teacher):
    nq, nt, feat = hidden.shape
    dv = proj.shape[1]
    slots, pass_tokens, _ = passages.shape
    n = lax.axis_size("shard")
    half_q = nq // 2
    rows = half_q * nt
    requests = cand_owner.size
    cap = max(8, 2 * max(2, (2 * requests + n - 1) // n))
    slot_bits = slots.bit_length()
    query_bits = max(1, (half_q - 1).bit_length())
    width = -(-(n * half_q) // LANES) * LANES
    flat_h = hidden.reshape(nq * nt, feat)

    query = jnp.broadcast_to(jnp.arange(nq)[:, None], teacher.shape)
    code = (
        cand_slot.reshape(teacher.shape)
        + 1
        + ((query % half_q) << slot_bits)
        + (query_len[:, None] << (slot_bits + query_bits))
    )
    zero = jnp.zeros((requests,), F32)
    meta = jnp.stack(
        [
            cand_owner.reshape(-1).astype(F32),
            code.reshape(-1).astype(F32),
            teacher.reshape(-1),
            query.reshape(-1).astype(F32),
            zero, zero, zero, zero,
        ]
    )
    vmem = pl.BlockSpec(memory_space=pltpu.VMEM)
    smem = pl.BlockSpec(memory_space=pltpu.SMEM)
    dma = pltpu.SemaphoreType.DMA
    shape = jax.ShapeDtypeStruct
    q_all, pin, tab, codes, info = pl.pallas_call(
        functools.partial(request_kernel, n, half_q, nt),
        out_shape=(
            shape((n, rows, dv), BF16),
            shape((rows, dv), F32),
            shape((n, 8, LANES), F32),
            shape((n, LANES), jnp.int32),
            shape((8, LANES), F32),
        ),
        in_specs=[vmem] * 3,
        out_specs=(vmem,) * 5,
        scratch_shapes=[
            pltpu.VMEM((nq * nt, dv), F32),
            pltpu.VMEM((rows, dv), F32),
            pltpu.VMEM((8, requests), F32),
            pltpu.VMEM((n, 8, LANES), F32),
            dma((2,)), dma((2,)), dma((n,)), dma((n,)), dma((n,)), dma((n,)),
        ],
        compiler_params=pltpu.CompilerParams(
            collective_id=0, has_side_effects=True, vmem_limit_bytes=32 << 20
        ),
        name="requests",
    )(flat_h, proj, meta)

    a_part, t_part, stat = pl.pallas_call(
        functools.partial(score_kernel, n, half_q, nt, slot_bits, query_bits, cap),
        out_shape=(
            shape((n * half_q, nt, dv), F32),
            shape((n * half_q, nt, dv), F32),
            shape((8, width), F32),
        ),
        in_specs=[smem, smem, vmem, vmem, pl.BlockSpec(memory_space=pl.ANY)],
        out_specs=(vmem,) * 3,
        scratch_shapes=[
            pltpu.VMEM((slots, pass_tokens, dv), BF16),
            pltpu.VMEM((cap, nt, dv), F32),
            pltpu.VMEM((cap, LANES), F32),
            pltpu.VMEM((2 * half_q, cap, LANES), F32),
            dma,
        ],
        compiler_params=pltpu.CompilerParams(vmem_limit_bytes=48 << 20),
        name="scores",
    )(codes, pass_len, q_all, tab, passages)

    inside = feat % n == 0 and (feat // n) % 8 == 0
    piece = feat // n if inside else 8
    kl, gh, gp = pl.pallas_call(
        functools.partial(grad_kernel, n, half_q, nt, inside),
        out_shape=(
            shape((8, LANES), F32),
            shape((nq * nt, feat), BF16),
            shape((feat, dv), F32),
        ),
        in_specs=[smem] + [vmem] * 7,
        out_specs=(vmem,) * 3,
        scratch_shapes=[
            pltpu.VMEM((n, 8, width), F32),
            pltpu.VMEM((n * half_q, LANES), F32),
            pltpu.VMEM((n, rows, dv), BF16),
            pltpu.VMEM((n, rows, dv), BF16),
            pltpu.VMEM((nq * nt, dv), BF16),
            pltpu.VMEM((2, 8, LANES), F32),
            pltpu.VMEM((feat, dv), F32),
            pltpu.VMEM((n, piece, dv), F32),
            dma((2,)), dma((2,)),
        ]
        + [dma((n,))] * 8,
        compiler_params=pltpu.CompilerParams(
            collective_id=1, has_side_effects=True, vmem_limit_bytes=48 << 20
        ),
        name="grads",
    )(query_len, a_part, t_part, stat, pin, info, flat_h, proj)
    if not inside:
        gp = lax.psum(gp, "shard")
    return kl[0, :nq], gh.reshape(nq, nt, feat), gp


def solution(mesh):
    in_specs = (
        P("shard", None, "section"),
        P("section", None),
        P("shard", None, None),
        P("shard"),
        P("shard"),
        P("section", "shard", None, None),
        P("section", "shard", None),
        P("shard", "section"),
    )
    out_specs = (P("shard"), P("shard", None, "section"), P("section", None))
    return jax.shard_map(local, mesh=mesh, in_specs=in_specs, out_specs=out_specs, check_vma=False)
```

time: 553 us -> 152 us (0.27)
  waiting for transfers between devices: 384 us -> 0 us
  Pallas kernels: 0 us -> 134 us
  local copies, waits for them, and re-layouts: 99.4 us -> 14 us
  blocking collectives: 17.8 us -> 0 us
  matrix products: 15.1 us -> 0 us
  between operations: 14.6 us -> 0.7 us
  starting transfers between devices: 10.4 us -> 0 us
  other arithmetic: 10.1 us -> 2.14 us
    psum x3 -> x0, waiting for transfers between devices: 195 us -> none  [the longest x1 110 us: local(): grad_proj = lax.psum(local_proj, 'shard')]
    all_to_all x2 -> x0, waiting for transfers between devices: 189 us -> none  [the longest x1 189 us: local(): lax.all_to_all(out_blocks, 'shard', split_axis=0, concat_axis=0, tiled=True)]
    pallas_call x0 -> x3, Pallas kernels: none -> 134 us  [the longest x1 90 us: local(): pl.pallas_call(functools.partial(score_kernel, n, half_q, nt, slot_bits,...]
    gather x6 -> x0, local copies, waits for them, and re-layouts: 60.9 us -> none  [the longest x1 48 us: local(): passages[wanted].reshape(owners, capacity, pass_tokens, vec_dim)]
    all_to_all x1 -> x0, blocking collectives: 15.4 us -> none  [local(): lax.all_to_all(slot_table, 'shard', split_axis=0, concat_axis=0, tiled=True)]
    dot_general x5 -> x0, matrix products: 15.1 us -> none  [the longest x1 6.63 us: token_scores(): jnp.einsum('bid,btd->bit', q_rows, blocks, preferred_element_type=jnp.flo...]
    all_to_all x2 -> x0, local copies, waits for them, and re-layouts: 13 us -> none  [the longest x1 12.3 us: local(): lax.all_to_all(out_blocks, 'shard', split_axis=0, concat_axis=0, tiled=True)]
    reshape x6 -> x0, local copies, waits for them, and re-layouts: 11.7 us -> none  [the longest x1 10.7 us: local(): passages[wanted].reshape(owners, capacity, pass_tokens, vec_dim)]
  transfers between devices with their start and end apart: 5 -> 0, of which waited for: 4 -> 0; matrix products, arithmetic and copies ran while one was open for 12% -> 0% of each run, Pallas kernels for 0% -> 0%
where the time goes in v1:
time: 152 us; the launch traced here: 151 us
  Pallas kernels  134 us (88%)
  local copies, waits for them, and re-layouts  14 us (9%)
  other arithmetic  2.14 us (1%)
    pallas_call x1, Pallas kernels, local(): pl.pallas_call(functools.partial(score_kernel, n, half_q, nt, slot_bits,...  90 us
    pallas_call x1, Pallas kernels, local(): pl.pallas_call(functools.partial(grad_kernel, n, half_q, nt, inside), out...  29 us
    pallas_call x1, Pallas kernels, local(): pl.pallas_call(functools.partial(request_kernel, n, half_q, nt), out_shap...  15.5 us
    unnamed x15, local copies, waits for them, and re-layouts  12.2 us

profile of v1, /device:TPU:0, one launch (start us, length us, event | category | flops | bytes accessed | tf_op | source)
XLA Modules:
  0.0 151.3 jit_solution(14907088523906230989)
XLA Ops:
  0.6 0.8 stack_reshape.3
  1.4 0.7 broadcast_shift-left_fusion
  2.1 0.1 select_shift-left_fusion
  2.1 0.1 shift_left.23
  2.2 0.1 add.58
  2.3 0.1 add.59
  2.4 0.7 convert_reduce_fusion
  3.1 0.1 convert_element_type.37
  3.2 0.7 broadcast_add_fusion
  3.9 0.1 add.55
  4.0 0.1 convert_element_type.40
  4.1 0.0 copy-start
  4.1 0.9 copy-done
  5.0 0.0 copy-start.2
  5.0 0.9 copy-done.2
  5.9 0.0 copy-start.4
  5.9 15.5 %requests.1 = (bf16[16,64,128]{2,1,0:T(8,128)(2,1)S(1)}, f32[64,128]{1,0:T(8,128)S(1)}, f32[16,8,128]{2,1,0:T(8,128)S(1)}, s32[16,128]{1,0:T(8,128)S(1)}, f32[8,128]{1,0:T(8,128)S(1)}) custom-call(bf16[128,384]{1,0:T(8,128)(2,1)S(1)} %bitcast.4, bf16[384,128]{1,0:T(8,128)(2,1)S(1)} %copy-done.2, f32[8,128]{1,0:T(8,128)S(1)} %stack.10.meta_ref), custom_call_target="tpu_custom_call" | custom-call | tf_op jit(solution)/shard_map/requests/pallas_call | solution.py:352
  21.3 9.0 %copy.11.pas_hbm = bf16[128,180,128]{2,1,0:T(8,128)(2,1)} copy(bf16[128,180,128]{2,0,1:T(8,128)(2,1)} %param.10) | data formatting | bytes 11796480 | tf_op args[2]
  30.4 0.0 copy-done.4
  30.4 0.0 copy-start.1
  30.4 0.0 copy-start.3
  30.4 0.0 copy-start.5
  30.4 90.0 %scores.1 = (f32[32,32,128]{2,1,0:T(8,128)S(1)}, f32[32,32,128]{2,1,0:T(8,128)S(1)}, f32[8,128]{1,0:T(8,128)S(1)}) custom-call(s32[16,128]{1,0:T(8,128)S(1)} %get-tuple-element.14.code, s32[128]{0:T(128)S(1)} %copy-done.4, bf16[16,64,128]{2,1,0:T(8,128)(2,1)S(1)} %get-tuple-element.15.q_ref, f32[16,8,128]{2,1,0:T(8,128)S(1)} %get-tuple-element.16.tab_ref, ...), custom_call_target="tpu_custom_call" | custom-call | tf_op jit(solution)/shard_map/scores/pallas_call | solution.py:376
  120.4 0.0 copy-done.1
  120.4 0.0 copy-done.3
  120.4 0.0 copy-done.5
  120.4 29.0 %grads.1 = (f32[8,128]{1,0:T(8,128)S(1)}, bf16[128,384]{1,0:T(8,128)(2,1)S(1)}, f32[384,128]{1,0:T(8,128)S(1)}) custom-call(s32[4]{0:T(128)S(1)} %copy-done.5, f32[32,32,128]{2,1,0:T(8,128)S(1)} %get-tuple-element.17.a_ref, f32[32,32,128]{2,1,0:T(8,128)S(1)} %get-tuple-element.18.t_ref, f32[8,128]{1,0:T(8,128)S(1)} %get-tuple-element.19.stat_ref, ...), custom_call_target="tpu_custom_call" | custom-call | tf_op jit(solution)/shard_map/grads/pallas_call | solution.py:398
  149.5 0.5 slice_bitcast_fusion
  150.0 0.6 copy.14
  150.6 0.7 copy.15
  (6 shorter events, 0.0 us)
Async XLA Ops:
  4.1 0.9 copy-start
  5.0 0.9 copy-start.2
  5.9 24.5 %copy-start.4 = (s32[128]{0:T(128)S(1)}, s32[128]{0:T(128)}, u32[]{:S(2)}) copy-start(s32[128]{0:T(128)} %plen.1) | copy-start | bytes 1540
  30.4 90.0 %copy-start.1 = (bf16[4,32,384]{2,1,0:T(8,128)(2,1)S(1)}, bf16[4,32,384]{2,1,0:T(8,128)(2,1)}, u32[]{:S(2)}) copy-start(bf16[4,32,384]{2,1,0:T(8,128)(2,1)} %param.8) | copy-start | bytes 294916
  30.4 90.0 %copy-start.3 = (bf16[384,128]{1,0:T(8,128)(2,1)S(1)}, bf16[384,128]{1,0:T(8,128)(2,1)}, u32[]{:S(2)}) copy-start(bf16[384,128]{1,0:T(8,128)(2,1)} %p_ref.3) | copy-start | bytes 294916
  30.4 90.0 %copy-start.5 = (s32[4]{0:T(128)S(1)}, s32[4]{0:T(128)}, u32[]{:S(2)}) copy-start(s32[4]{0:T(128)} %qlen.1) | copy-start | bytes 52

commit v2 on v1

--- a/solution.py
+++ b/solution.py
@@ -12,7 +12,8 @@
 EPSILON = 1e-06
 NEGATIVE = -1e30
 LANES = 128
-GROUP = 4
+GROUP = 8
+CHUNK = 64
 F32 = jnp.float32
 BF16 = jnp.bfloat16
 MESH = pl.DeviceIdType.MESH
@@ -52,8 +53,8 @@
 
 def request_kernel(
     n, half_q, nt, h_ref, p_ref, meta_ref,
-    q_out, pin_out, tab_out, code_out, info_out,
-    part, opart, ometa, tab,
+    q_out, pin_out, code_out, prob_out, teach_out, info_out,
+    tab_out, part, opart, ometa, tab,
     sib_send, sib_recv, st, rt, sq, rq,
 ):
     sec, me = lax.axis_index("section"), lax.axis_index("shard")
@@ -115,97 +116,128 @@
     count = jnp.sum(got[:, 3, :], axis=1, keepdims=True)
     codes = jnp.where(iota((n, LANES), 1) == LANES - 1, count, got[:, 0, :])
     code_out[...] = (codes + 0.5).astype(jnp.int32)
+    prob_out[...] = got[:, 1, :]
+    teach_out[...] = got[:, 2, :]
     each_peer(n, me, lambda p, i: remote(
         q_out.at[me], q_out.at[p], sq.at[i], rq.at[p], shard=p).wait())
 
 
 def score_kernel(
-    n, half_q, nt, slot_bits, query_bits, cap,
-    code, plen, q_ref, tab_ref, pas_hbm, a_out, t_out, stat_out,
-    pas, u_ref, stud_ref, coef_ref, sem,
+    n, half_q, nt, slot_bits, query_bits,
+    code, prob, teach, plen, q_ref, pas_hbm, a_out, t_out, stat_out,
+    pas, u_ref, stud_ref, own_ref, prob_ref, teach_ref, coef_ref, listing, sem,
 ):
     load = pltpu.make_async_copy(pas_hbm, pas, sem)
     load.start()
     pass_tokens = pas.shape[1]
     scale = SHARPNESS * math.log2(math.e)
-    stat_out[...] = jnp.where(iota(stat_out.shape, 0) == 0, NEGATIVE, 0.0)
-    load.wait()
+    len_bits = nt.bit_length()
+    high = slot_bits + query_bits + len_bits
+
+    def per_source(q, start):
+        cnt = code[q, LANES - 1]
+
+        def eight(g, carry):
+            for k in range(8):
+                r = g * 8 + k
+                e = start + r
+                listing[e] = code[q, r] | lax.shift_left(q, high)
+                prob_ref[pl.ds(e, 1), :] = jnp.full((1, LANES), prob[q, r], F32)
+                teach_ref[pl.ds(e, 1), :] = jnp.full((1, LANES), teach[q, r], F32)
+            return carry
+
+        lax.fori_loop(0, lax.shift_right_logical(cnt + 7, 3), eight, 0)
+        return start + cnt
+
+    count = lax.fori_loop(0, n, per_source, 0)
+    for k in range(GROUP):
+        listing[count + k] = 0
+    groups = lax.div(count + (GROUP - 1), GROUP)
     tok = iota((nt, pass_tokens), 1)
     tok_row = iota((nt, 1), 0)
 
-    def per_source(q, carry):
-        cnt = code[q, LANES - 1]
-        groups = lax.div(cnt + (GROUP - 1), GROUP)
-
-        def group(g, carry):
-            for k in range(GROUP):
-                r = g * GROUP + k
-                c = code[q, r]
-                slot = jnp.maximum((c & ((1 << slot_bits) - 1)) - 1, 0)
-                which = lax.shift_right_logical(c, slot_bits) & ((1 << query_bits) - 1)
-                qlen = lax.shift_right_logical(c, slot_bits + query_bits)
-                block = pas[slot]
-                vecs = q_ref[q, pl.ds(pl.multiple_of(which * nt, nt), nt), :]
-                logits = lax.dot_general(
-                    vecs, block, (((1,), (1,)), ((), ())), preferred_element_type=F32
-                )
-                logits = jnp.where(tok < plen[slot], logits * scale, NEGATIVE)
-                top = jnp.max(logits, axis=1, keepdims=True)
-                terms = jnp.exp2(logits - top)
-                total = jnp.sum(terms, axis=1, keepdims=True)
-                best = top * (math.log(2.0) / SHARPNESS) + jnp.log(total) * (1.0 / SHARPNESS)
-                student = jnp.sum(jnp.where(tok_row < qlen, best, 0.0), axis=0, keepdims=True)
-                unit = jnp.dot(terms.astype(BF16), block, preferred_element_type=F32)
-                u_ref[r] = unit * (1.0 / total)
-                stud_ref[pl.ds(r, 1), :] = jnp.broadcast_to(student, (1, LANES))
-            return carry
-
-        lax.fori_loop(0, groups, group, 0)
-        stud = stud_ref[...]
-        row_id, lane_id = iota((cap, LANES), 0), iota((cap, LANES), 1)
-        table = tab_ref[q]
-
-        def column(v):
-            return jnp.sum(
-                jnp.where(row_id == lane_id, table[v : v + 1, :], 0.0), axis=1, keepdims=True
+    def place(c):
+        which = lax.shift_right_logical(c, slot_bits) & ((1 << query_bits) - 1)
+        return lax.shift_right_logical(c, high), which
+
+    load.wait()
+
+    def group(g, carry):
+        for k in range(GROUP):
+            e = g * GROUP + k
+            c = listing[e]
+            slot = jnp.maximum((c & ((1 << slot_bits) - 1)) - 1, 0)
+            q, which = place(c)
+            qlen = lax.shift_right_logical(c, slot_bits + query_bits) & ((1 << len_bits) - 1)
+            block = pas[slot]
+            vecs = q_ref[q, pl.ds(pl.multiple_of(which * nt, nt), nt), :]
+            logits = lax.dot_general(
+                vecs, block, (((1,), (1,)), ((), ())), preferred_element_type=F32
             )
-
-        codes = (column(0) + 0.5).astype(jnp.int32)
-        prob, teach = column(1), column(2)
-        which = lax.shift_right_logical(codes, slot_bits) & ((1 << query_bits) - 1)
-        stat = stat_out[...]
-        stat_row, stat_lane = iota(stat.shape, 0), iota(stat.shape, 1)
-        for j in range(half_q):
-            mask = (row_id < cnt) & (which == j)
-            top = jnp.max(jnp.where(mask, stud, NEGATIVE), axis=0, keepdims=True)
-            terms = jnp.where(mask, jnp.exp(jnp.where(mask, stud - top, 0.0)), 0.0)
-            total = jnp.sum(terms, axis=0, keepdims=True)
-            cross = jnp.sum(jnp.where(mask, prob * (teach - stud), 0.0), axis=0, keepdims=True)
-            coef_ref[j] = terms
-            coef_ref[half_q + j] = jnp.where(mask, jnp.broadcast_to(prob, (cap, LANES)), 0.0)
-            new = jnp.where(
-                stat_row == 0, top[:, :1], jnp.where(stat_row == 1, total[:, :1], cross[:, :1])
-            )
-            stat = jnp.where((stat_lane == q * half_q + j) & (stat_row < 3), new, stat)
-        stat_out[...] = stat
-
-        def gather(g, sums):
-            for k in range(GROUP):
-                r = g * GROUP + k
-                unit = u_ref[r]
-                sums = tuple(
-                    one + coef_ref[at, pl.ds(r, 1), :] * unit for at, one in enumerate(sums)
-                )
-            return sums
-
-        zero = jnp.zeros(u_ref.shape[1:], F32)
-        sums = lax.fori_loop(0, groups, gather, (zero,) * (2 * half_q))
-        for j in range(half_q):
-            a_out[q * half_q + j] = sums[j]
-            t_out[q * half_q + j] = sums[half_q + j]
+            logits = jnp.where(tok < plen[slot], logits * scale, NEGATIVE)
+            top = jnp.max(logits, axis=1, keepdims=True)
+            terms = jnp.exp2(logits - top)
+            total = jnp.sum(terms, axis=1, keepdims=True)
+            best = top * (math.log(2.0) / SHARPNESS) + jnp.log(total) * (1.0 / SHARPNESS)
+            student = jnp.sum(jnp.where(tok_row < qlen, best, 0.0), axis=0, keepdims=True)
+            unit = jnp.dot(terms.astype(BF16), block, preferred_element_type=F32)
+            u_ref[e] = unit * (1.0 / total)
+            stud_ref[pl.ds(e, 1), :] = jnp.broadcast_to(student, (1, LANES))
+            own_ref[pl.ds(e, 1), :] = jnp.full((1, LANES), q * half_q + which, jnp.int32)
         return carry
 
-    lax.fori_loop(0, n, per_source, 0)
+    lax.fori_loop(0, groups, group, 0)
+
+    width = stat_out.shape[1]
+    chunks = lax.div(count + (CHUNK - 1), CHUNK)
+
+    def wide(x):
+        return x if width == LANES else jnp.concatenate([x] * (width // LANES), axis=1)
+
+    def chunk(c):
+        at = pl.ds(pl.multiple_of(c * CHUNK, CHUNK), CHUNK)
+        valid = iota((CHUNK, 1), 0) + c * CHUNK < count
+        mask = (wide(own_ref[at, :]) == iota((CHUNK, width), 1)) & valid
+        return at, valid, mask, stud_ref[at, :]
+
+    def find_top(c, top):
+        at, valid, mask, stud = chunk(c)
+        return jnp.maximum(
+            top, jnp.max(jnp.where(mask, wide(stud), NEGATIVE), axis=0, keepdims=True)
+        )
+
+    none = jnp.zeros((1, width), F32)
+    top = lax.fori_loop(0, chunks, find_top, none + NEGATIVE)
+
+    def weigh(c, sums):
+        at, valid, mask, stud = chunk(c)
+        mine = jnp.max(jnp.where(mask, top, NEGATIVE), axis=1, keepdims=True)
+        terms = jnp.where(valid, jnp.exp(jnp.where(valid, stud - mine, 0.0)), 0.0)
+        likely = jnp.where(valid, prob_ref[at, :], 0.0)
+        coef_ref[at, :] = terms
+        cross = jnp.where(valid, likely * (teach_ref[at, :] - stud), 0.0)
+        prob_ref[at, :] = likely
+        return (
+            sums[0] + jnp.sum(jnp.where(mask, wide(terms), 0.0), axis=0, keepdims=True),
+            sums[1] + jnp.sum(jnp.where(mask, wide(cross), 0.0), axis=0, keepdims=True),
+        )
+
+    total, cross = lax.fori_loop(0, chunks, weigh, (none, none))
+    stat_out[...] = jnp.concatenate([top, total, cross, jnp.zeros((5, width), F32)], axis=0)
+    a_out[...] = jnp.zeros_like(a_out)
+    t_out[...] = jnp.zeros_like(t_out)
+
+    def gather(g, carry):
+        for k in range(4):
+            e = g * 4 + k
+            q, which = place(listing[e])
+            at = q * half_q + which
+            unit = u_ref[e]
+            a_out[at] += coef_ref[pl.ds(e, 1), :] * unit
+            t_out[at] += prob_ref[pl.ds(e, 1), :] * unit
+        return carry
+
+    lax.fori_loop(0, lax.shift_right_logical(count + 3, 2), gather, 0)
 
 
 def grad_kernel(
@@ -322,7 +354,8 @@
     half_q = nq // 2
     rows = half_q * nt
     requests = cand_owner.size
-    cap = max(8, 2 * max(2, (2 * requests + n - 1) // n))
+    cap = 2 * max(2, (2 * requests + n - 1) // n)
+    most = -(-(n * cap + 8) // CHUNK) * CHUNK
     slot_bits = slots.bit_length()
     query_bits = max(1, (half_q - 1).bit_length())
     width = -(-(n * half_q) // LANES) * LANES
@@ -349,18 +382,20 @@
     smem = pl.BlockSpec(memory_space=pltpu.SMEM)
     dma = pltpu.SemaphoreType.DMA
     shape = jax.ShapeDtypeStruct
-    q_all, pin, tab, codes, info = pl.pallas_call(
+    q_all, pin, codes, probs, teachs, info = pl.pallas_call(
         functools.partial(request_kernel, n, half_q, nt),
         out_shape=(
             shape((n, rows, dv), BF16),
             shape((rows, dv), F32),
-            shape((n, 8, LANES), F32),
             shape((n, LANES), jnp.int32),
+            shape((n, LANES), F32),
+            shape((n, LANES), F32),
             shape((8, LANES), F32),
         ),
         in_specs=[vmem] * 3,
-        out_specs=(vmem,) * 5,
+        out_specs=(vmem,) * 6,
         scratch_shapes=[
+            pltpu.VMEM((n, 8, LANES), F32),
             pltpu.VMEM((nq * nt, dv), F32),
             pltpu.VMEM((rows, dv), F32),
             pltpu.VMEM((8, requests), F32),
@@ -374,24 +409,28 @@
     )(flat_h, proj, meta)
 
     a_part, t_part, stat = pl.pallas_call(
-        functools.partial(score_kernel, n, half_q, nt, slot_bits, query_bits, cap),
+        functools.partial(score_kernel, n, half_q, nt, slot_bits, query_bits),
         out_shape=(
             shape((n * half_q, nt, dv), F32),
             shape((n * half_q, nt, dv), F32),
             shape((8, width), F32),
         ),
-        in_specs=[smem, smem, vmem, vmem, pl.BlockSpec(memory_space=pl.ANY)],
+        in_specs=[smem] * 4 + [vmem, pl.BlockSpec(memory_space=pl.ANY)],
         out_specs=(vmem,) * 3,
         scratch_shapes=[
             pltpu.VMEM((slots, pass_tokens, dv), BF16),
-            pltpu.VMEM((cap, nt, dv), F32),
-            pltpu.VMEM((cap, LANES), F32),
-            pltpu.VMEM((2 * half_q, cap, LANES), F32),
+            pltpu.VMEM((most, nt, dv), F32),
+            pltpu.VMEM((most, LANES), F32),
+            pltpu.VMEM((most, LANES), jnp.int32),
+            pltpu.VMEM((most, LANES), F32),
+            pltpu.VMEM((most, LANES), F32),
+            pltpu.VMEM((most, LANES), F32),
+            pltpu.SMEM((most,), jnp.int32),
             dma,
         ],
         compiler_params=pltpu.CompilerParams(vmem_limit_bytes=48 << 20),
         name="scores",
-    )(codes, pass_len, q_all, tab, passages)
+    )(codes, probs, teachs, pass_len, q_all, passages)
 
     inside = feat % n == 0 and (feat // n) % 8 == 0
     piece = feat // n if inside else 8

time: 152 us -> 140 us (0.921)
  Pallas kernels: 134 us -> 123 us
    pallas_call x1, Pallas kernels: 90 us -> 41.4 us  [local(): pl.pallas_call(functools.partial(score_kernel, n, half_q, nt, slot_bits,...]
    pallas_call x1, Pallas kernels: 29 us -> 66.6 us  [local(): pl.pallas_call(functools.partial(grad_kernel, n, half_q, nt, inside), out...]
where the time goes in v2:
time: 140 us
  Pallas kernels  123 us (88%)
  local copies, waits for them, and re-layouts  14 us (10%)
  other arithmetic  2.14 us (2%)
    pallas_call x1, Pallas kernels, local(): pl.pallas_call(functools.partial(grad_kernel, n, half_q, nt, inside), out...  66.6 us
    pallas_call x1, Pallas kernels, local(): pl.pallas_call(functools.partial(score_kernel, n, half_q, nt, slot_bits,...  41.4 us
    pallas_call x1, Pallas kernels, local(): pl.pallas_call(functools.partial(request_kernel, n, half_q, nt), out_shap...  15.5 us
    unnamed x15, local copies, waits for them, and re-layouts  12.2 us

profile of v2, /device:TPU:0, one launch (start us, length us, event | category | flops | bytes accessed | tf_op | source)
XLA Modules:
  0.0 140.2 jit_solution(7629976726122549118)
XLA Ops:
  0.6 0.8 stack_reshape.3
  1.4 0.7 broadcast_shift-left_fusion
  2.1 0.1 select_shift-left_fusion
  2.1 0.1 shift_left.23
  2.2 0.1 add.58
  2.3 0.1 add.59
  2.4 0.7 convert_reduce_fusion
  3.1 0.1 convert_element_type.37
  3.2 0.7 broadcast_add_fusion
  3.9 0.1 add.55
  4.0 0.1 convert_element_type.40
  4.1 0.0 copy-start
  4.1 0.9 copy-done
  5.0 0.0 copy-start.2
  5.0 0.9 copy-done.2
  5.9 0.0 copy-start.4
  5.9 15.5 %requests.1 = (bf16[16,64,128]{2,1,0:T(8,128)(2,1)S(1)}, f32[64,128]{1,0:T(8,128)S(1)}, s32[16,128]{1,0:T(8,128)S(1)}, f32[16,128]{1,0:T(8,128)S(1)}, f32[16,128]{1,0:T(8,128)S(1)}, /*index=5*/f32[8,128]{1,0:T(8,128)S(1)}) custom-call(bf16[128,384]{1,0:T(8,128)(2,1)S(1)} %bitcast.4, bf16[384,128]{1,0:T(8,128)(2,1)S(1)} %copy-done.2, f32[8,128]{1,0:T(8,128)S(1)} %stack.10.meta_ref), custom_call_target="tpu_custom_call" | custom-call | tf_op jit(solution)/shard_map/requests/pallas_call | solution.py:385
  21.3 9.0 %copy.11.pas_hbm = bf16[128,180,128]{2,1,0:T(8,128)(2,1)} copy(bf16[128,180,128]{2,0,1:T(8,128)(2,1)} %param.10) | data formatting | bytes 11796480 | tf_op args[2]
  30.4 0.0 copy-done.4
  30.4 0.0 copy-start.1
  30.4 0.0 copy-start.3
  30.4 0.0 copy-start.5
  30.4 41.4 %scores.1 = (f32[32,32,128]{2,1,0:T(8,128)S(1)}, f32[32,32,128]{2,1,0:T(8,128)S(1)}, f32[8,128]{1,0:T(8,128)S(1)}) custom-call(s32[16,128]{1,0:T(8,128)S(1)} %get-tuple-element.15.code, f32[16,128]{1,0:T(8,128)S(1)} %get-tuple-element.16.prob, f32[16,128]{1,0:T(8,128)S(1)} %get-tuple-element.17.teach, s32[128]{0:T(128)S(1)} %copy-done.4, ...), custom_call_target="tpu_custom_call" | custom-call | tf_op jit(solution)/shard_map/scores/pallas_call | solution.py:411
  71.8 0.0 copy-done.1
  71.8 0.0 copy-done.3
  71.8 0.0 copy-done.5
  71.8 66.6 %grads.1 = (f32[8,128]{1,0:T(8,128)S(1)}, bf16[128,384]{1,0:T(8,128)(2,1)S(1)}, f32[384,128]{1,0:T(8,128)S(1)}) custom-call(s32[4]{0:T(128)S(1)} %copy-done.5, f32[32,32,128]{2,1,0:T(8,128)S(1)} %get-tuple-element.19.a_ref, f32[32,32,128]{2,1,0:T(8,128)S(1)} %get-tuple-element.20.t_ref, f32[8,128]{1,0:T(8,128)S(1)} %get-tuple-element.21.stat_ref, ...), custom_call_target="tpu_custom_call" | custom-call | tf_op jit(solution)/shard_map/grads/pallas_call | solution.py:437
  138.4 0.5 slice_bitcast_fusion
  138.9 0.6 copy.14
  139.5 0.7 copy.15
  (6 shorter events, 0.0 us)
Async XLA Ops:
  4.1 0.9 copy-start
  5.0 0.9 copy-start.2
  5.9 24.5 %copy-start.4 = (s32[128]{0:T(128)S(1)}, s32[128]{0:T(128)}, u32[]{:S(2)}) copy-start(s32[128]{0:T(128)} %plen.1) | copy-start | bytes 1540
  30.4 41.4 %copy-start.1 = (bf16[4,32,384]{2,1,0:T(8,128)(2,1)S(1)}, bf16[4,32,384]{2,1,0:T(8,128)(2,1)}, u32[]{:S(2)}) copy-start(bf16[4,32,384]{2,1,0:T(8,128)(2,1)} %param.8) | copy-start | bytes 294916
  30.4 41.4 %copy-start.3 = (bf16[384,128]{1,0:T(8,128)(2,1)S(1)}, bf16[384,128]{1,0:T(8,128)(2,1)}, u32[]{:S(2)}) copy-start(bf16[384,128]{1,0:T(8,128)(2,1)} %p_ref.3) | copy-start | bytes 294916
  30.4 41.4 %copy-start.5 = (s32[4]{0:T(128)S(1)}, s32[4]{0:T(128)}, u32[]{:S(2)}) copy-start(s32[4]{0:T(128)} %qlen.1) | copy-start | bytes 52

commit v3 on v2

--- a/solution.py
+++ b/solution.py
@@ -125,7 +125,7 @@
 def score_kernel(
     n, half_q, nt, slot_bits, query_bits,
     code, prob, teach, plen, q_ref, pas_hbm, a_out, t_out, stat_out,
-    pas, u_ref, stud_ref, own_ref, prob_ref, teach_ref, coef_ref, listing, sem,
+    pas, turned, u_ref, stud_ref, own_ref, prob_ref, teach_ref, coef_ref, listing, sem,
 ):
     load = pltpu.make_async_copy(pas_hbm, pas, sem)
     load.start()
@@ -153,37 +153,60 @@
     for k in range(GROUP):
         listing[count + k] = 0
     groups = lax.div(count + (GROUP - 1), GROUP)
-    tok = iota((nt, pass_tokens), 1)
-    tok_row = iota((nt, 1), 0)
+    side = LANES // nt
+    tok = iota((pass_tokens, LANES), 0)
+    lane = iota((1, LANES), 1)
+    piece = iota((LANES, LANES), 1)
 
     def place(c):
         which = lax.shift_right_logical(c, slot_bits) & ((1 << query_bits) - 1)
         return lax.shift_right_logical(c, high), which
 
+    def turn(q, carry):
+        for j in range(half_q):
+            vecs = q_ref[q, j * nt : (j + 1) * nt, :].astype(F32)
+            turned[q * half_q + j] = jnp.concatenate([vecs] * side, axis=0).T.astype(BF16)
+        return carry
+
+    lax.fori_loop(0, n, turn, 0)
     load.wait()
 
     def group(g, carry):
-        for k in range(GROUP):
-            e = g * GROUP + k
-            c = listing[e]
-            slot = jnp.maximum((c & ((1 << slot_bits) - 1)) - 1, 0)
-            q, which = place(c)
-            qlen = lax.shift_right_logical(c, slot_bits + query_bits) & ((1 << len_bits) - 1)
-            block = pas[slot]
-            vecs = q_ref[q, pl.ds(pl.multiple_of(which * nt, nt), nt), :]
-            logits = lax.dot_general(
-                vecs, block, (((1,), (1,)), ((), ())), preferred_element_type=F32
+        for first in range(0, GROUP, side):
+            blocks, weights, owners = [], [], []
+            limit, tokens = jnp.zeros((1, LANES), jnp.int32), jnp.zeros((1, LANES), jnp.int32)
+            for k in range(side):
+                c = listing[g * GROUP + first + k]
+                slot = jnp.maximum((c & ((1 << slot_bits) - 1)) - 1, 0)
+                q, which = place(c)
+                qlen = lax.shift_right_logical(c, slot_bits + query_bits) & ((1 << len_bits) - 1)
+                owners.append(q * half_q + which)
+                blocks.append(pas[slot])
+                here = (piece >= k * nt) & (piece < (k + 1) * nt)
+                weights.append(jnp.where(here, turned[owners[k]], jnp.zeros((), BF16)))
+                here = lane >= k * nt
+                limit = jnp.where(here, plen[slot], limit)
+                tokens = jnp.where(here, qlen + k * nt, tokens)
+            logits = jnp.dot(
+                jnp.concatenate(blocks, axis=1), jnp.concatenate(weights, axis=0),
+                preferred_element_type=F32,
             )
-            logits = jnp.where(tok < plen[slot], logits * scale, NEGATIVE)
-            top = jnp.max(logits, axis=1, keepdims=True)
+            logits = jnp.where(tok < limit, logits * scale, NEGATIVE)
+            top = jnp.max(logits, axis=0, keepdims=True)
             terms = jnp.exp2(logits - top)
-            total = jnp.sum(terms, axis=1, keepdims=True)
+            total = jnp.sum(terms, axis=0, keepdims=True)
             best = top * (math.log(2.0) / SHARPNESS) + jnp.log(total) * (1.0 / SHARPNESS)
-            student = jnp.sum(jnp.where(tok_row < qlen, best, 0.0), axis=0, keepdims=True)
-            unit = jnp.dot(terms.astype(BF16), block, preferred_element_type=F32)
-            u_ref[e] = unit * (1.0 / total)
-            stud_ref[pl.ds(e, 1), :] = jnp.broadcast_to(student, (1, LANES))
-            own_ref[pl.ds(e, 1), :] = jnp.full((1, LANES), q * half_q + which, jnp.int32)
+            best = jnp.where(lane < tokens, best, 0.0)
+            shares = (terms * (1.0 / total)).T.astype(BF16)
+            for k in range(side):
+                e = g * GROUP + first + k
+                here = (lane >= k * nt) & (lane < (k + 1) * nt)
+                student = jnp.sum(jnp.where(here, best, 0.0), axis=1, keepdims=True)
+                u_ref[e] = jnp.dot(
+                    shares[k * nt : (k + 1) * nt, :], blocks[k], preferred_element_type=F32
+                )
+                stud_ref[pl.ds(e, 1), :] = jnp.broadcast_to(student, (1, LANES))
+                own_ref[pl.ds(e, 1), :] = jnp.full((1, LANES), owners[k], jnp.int32)
         return carry
 
     lax.fori_loop(0, groups, group, 0)
@@ -419,6 +442,7 @@
         out_specs=(vmem,) * 3,
         scratch_shapes=[
             pltpu.VMEM((slots, pass_tokens, dv), BF16),
+            pltpu.VMEM((n * half_q, dv, LANES), BF16),
             pltpu.VMEM((most, nt, dv), F32),
             pltpu.VMEM((most, LANES), F32),
             pltpu.VMEM((most, LANES), jnp.int32),

time: 140 us -> 98 us (0.70)
  Pallas kernels: 123 us -> 81 us
    pallas_call x1, Pallas kernels: 41.4 us -> 13.9 us  [local(): pl.pallas_call(functools.partial(score_kernel, n, half_q, nt, slot_bits,...]
    pallas_call x1, Pallas kernels: 66.6 us -> 51.6 us  [local(): pl.pallas_call(functools.partial(grad_kernel, n, half_q, nt, inside), out...]
where the time goes in v3:
time: 98 us; the launch traced here: 97.8 us
  Pallas kernels  81 us (83%)
  local copies, waits for them, and re-layouts  14 us (14%)
  other arithmetic  2.14 us (2%)
    pallas_call x1, Pallas kernels, local(): pl.pallas_call(functools.partial(grad_kernel, n, half_q, nt, inside), out...  51.6 us
    pallas_call x1, Pallas kernels, local(): pl.pallas_call(functools.partial(request_kernel, n, half_q, nt), out_shap...  15.5 us
    pallas_call x1, Pallas kernels, local(): pl.pallas_call(functools.partial(score_kernel, n, half_q, nt, slot_bits,...  13.9 us
    unnamed x15, local copies, waits for them, and re-layouts  12.2 us

profile of v3, /device:TPU:0, one launch (start us, length us, event | category | flops | bytes accessed | tf_op | source)
XLA Modules:
  0.0 97.8 jit_solution(412455152117173761)
XLA Ops:
  0.6 0.8 stack_reshape.3
  1.4 0.7 broadcast_shift-left_fusion
  2.1 0.1 select_shift-left_fusion
  2.1 0.1 shift_left.23
  2.2 0.1 add.58
  2.3 0.1 add.59
  2.4 0.7 convert_reduce_fusion
  3.1 0.1 convert_element_type.37
  3.2 0.7 broadcast_add_fusion
  3.9 0.1 add.55
  4.0 0.1 convert_element_type.40
  4.1 0.0 copy-start
  4.1 0.9 copy-done
  5.0 0.0 copy-start.2
  5.0 0.9 copy-done.2
  5.9 0.0 copy-start.4
  5.9 15.5 %requests.1 = (bf16[16,64,128]{2,1,0:T(8,128)(2,1)S(1)}, f32[64,128]{1,0:T(8,128)S(1)}, s32[16,128]{1,0:T(8,128)S(1)}, f32[16,128]{1,0:T(8,128)S(1)}, f32[16,128]{1,0:T(8,128)S(1)}, /*index=5*/f32[8,128]{1,0:T(8,128)S(1)}) custom-call(bf16[128,384]{1,0:T(8,128)(2,1)S(1)} %bitcast.4, bf16[384,128]{1,0:T(8,128)(2,1)S(1)} %copy-done.2, f32[8,128]{1,0:T(8,128)S(1)} %stack.10.meta_ref), custom_call_target="tpu_custom_call" | custom-call | tf_op jit(solution)/shard_map/requests/pallas_call | solution.py:408
  21.3 9.0 %copy.11.pas_hbm = bf16[128,180,128]{2,1,0:T(8,128)(2,1)} copy(bf16[128,180,128]{2,0,1:T(8,128)(2,1)} %param.10) | data formatting | bytes 11796480 | tf_op args[2]
  30.4 0.0 copy-done.4
  30.4 0.0 copy-start.1
  30.4 0.0 copy-start.3
  30.4 0.0 copy-start.5
  30.4 13.9 %scores.1 = (f32[32,32,128]{2,1,0:T(8,128)S(1)}, f32[32,32,128]{2,1,0:T(8,128)S(1)}, f32[8,128]{1,0:T(8,128)S(1)}) custom-call(s32[16,128]{1,0:T(8,128)S(1)} %get-tuple-element.15.code, f32[16,128]{1,0:T(8,128)S(1)} %get-tuple-element.16.prob, f32[16,128]{1,0:T(8,128)S(1)} %get-tuple-element.17.teach, s32[128]{0:T(128)S(1)} %copy-done.4, ...), custom_call_target="tpu_custom_call" | custom-call | tf_op jit(solution)/shard_map/scores/pallas_call | solution.py:434
  44.3 0.0 copy-done.1
  44.3 0.0 copy-done.3
  44.3 0.0 copy-done.5
  44.3 51.6 %grads.1 = (f32[8,128]{1,0:T(8,128)S(1)}, bf16[128,384]{1,0:T(8,128)(2,1)S(1)}, f32[384,128]{1,0:T(8,128)S(1)}) custom-call(s32[4]{0:T(128)S(1)} %copy-done.5, f32[32,32,128]{2,1,0:T(8,128)S(1)} %get-tuple-element.19.a_ref, f32[32,32,128]{2,1,0:T(8,128)S(1)} %get-tuple-element.20.t_ref, f32[8,128]{1,0:T(8,128)S(1)} %get-tuple-element.21.stat_ref, ...), custom_call_target="tpu_custom_call" | custom-call | tf_op jit(solution)/shard_map/grads/pallas_call | solution.py:461
  96.0 0.5 slice_bitcast_fusion
  96.5 0.6 copy.14
  97.1 0.7 copy.15
  (6 shorter events, 0.0 us)
Async XLA Ops:
  4.1 0.9 copy-start
  5.0 0.9 copy-start.2
  5.9 24.5 %copy-start.4 = (s32[128]{0:T(128)S(1)}, s32[128]{0:T(128)}, u32[]{:S(2)}) copy-start(s32[128]{0:T(128)} %plen.1) | copy-start | bytes 1540
  30.4 13.9 %copy-start.1 = (bf16[4,32,384]{2,1,0:T(8,128)(2,1)S(1)}, bf16[4,32,384]{2,1,0:T(8,128)(2,1)}, u32[]{:S(2)}) copy-start(bf16[4,32,384]{2,1,0:T(8,128)(2,1)} %param.8) | copy-start | bytes 294916
  30.4 13.9 %copy-start.3 = (bf16[384,128]{1,0:T(8,128)(2,1)S(1)}, bf16[384,128]{1,0:T(8,128)(2,1)}, u32[]{:S(2)}) copy-start(bf16[384,128]{1,0:T(8,128)(2,1)} %p_ref.3) | copy-start | bytes 294916
  30.4 13.9 %copy-start.5 = (s32[4]{0:T(128)S(1)}, s32[4]{0:T(128)}, u32[]{:S(2)}) copy-start(s32[4]{0:T(128)} %qlen.1) | copy-start | bytes 52

commit v4 on v3

--- a/solution.py
+++ b/solution.py
@@ -12,7 +12,7 @@
 EPSILON = 1e-06
 NEGATIVE = -1e30
 LANES = 128
-GROUP = 8
+GROUP = 16
 CHUNK = 64
 F32 = jnp.float32
 BF16 = jnp.bfloat16
@@ -197,7 +197,7 @@
             total = jnp.sum(terms, axis=0, keepdims=True)
             best = top * (math.log(2.0) / SHARPNESS) + jnp.log(total) * (1.0 / SHARPNESS)
             best = jnp.where(lane < tokens, best, 0.0)
-            shares = (terms * (1.0 / total)).T.astype(BF16)
+            shares = (terms * (1.0 / total)).astype(BF16).T
             for k in range(side):
                 e = g * GROUP + first + k
                 here = (lane >= k * nt) & (lane < (k + 1) * nt)
@@ -378,7 +378,7 @@
     rows = half_q * nt
     requests = cand_owner.size
     cap = 2 * max(2, (2 * requests + n - 1) // n)
-    most = -(-(n * cap + 8) // CHUNK) * CHUNK
+    most = -(-(n * cap + GROUP) // CHUNK) * CHUNK
     slot_bits = slots.bit_length()
     query_bits = max(1, (half_q - 1).bit_length())
     width = -(-(n * half_q) // LANES) * LANES

time: 98 us -> 96.4 us (0.984)
  Pallas kernels: 81 us -> 79.1 us
    pallas_call x1, Pallas kernels: 51.6 us -> 49.8 us  [local(): pl.pallas_call(functools.partial(grad_kernel, n, half_q, nt, inside), out...]
where the time goes in v4:
time: 96.4 us; the launch traced here: 95.9 us
  Pallas kernels  79.1 us (82%)
  local copies, waits for them, and re-layouts  14 us (15%)
  other arithmetic  2.14 us (2%)
    pallas_call x1, Pallas kernels, local(): pl.pallas_call(functools.partial(grad_kernel, n, half_q, nt, inside), out...  49.8 us
    pallas_call x1, Pallas kernels, local(): pl.pallas_call(functools.partial(request_kernel, n, half_q, nt), out_shap...  15.5 us
    pallas_call x1, Pallas kernels, local(): pl.pallas_call(functools.partial(score_kernel, n, half_q, nt, slot_bits,...  13.9 us
    unnamed x15, local copies, waits for them, and re-layouts  12.2 us

profile of v4, /device:TPU:0, one launch (start us, length us, event | category | flops | bytes accessed | tf_op | source)
XLA Modules:
  0.0 95.9 jit_solution(11625739555805039135)
XLA Ops:
  0.6 0.8 stack_reshape.3
  1.4 0.7 broadcast_shift-left_fusion
  2.1 0.1 select_shift-left_fusion
  2.1 0.1 shift_left.23
  2.2 0.1 add.58
  2.3 0.1 add.59
  2.4 0.7 convert_reduce_fusion
  3.1 0.1 convert_element_type.37
  3.2 0.7 broadcast_add_fusion
  3.9 0.1 add.55
  4.0 0.1 convert_element_type.40
  4.1 0.0 copy-start
  4.1 0.9 copy-done
  5.0 0.0 copy-start.2
  5.0 0.9 copy-done.2
  5.9 0.0 copy-start.4
  5.9 15.5 %requests.1 = (bf16[16,64,128]{2,1,0:T(8,128)(2,1)S(1)}, f32[64,128]{1,0:T(8,128)S(1)}, s32[16,128]{1,0:T(8,128)S(1)}, f32[16,128]{1,0:T(8,128)S(1)}, f32[16,128]{1,0:T(8,128)S(1)}, /*index=5*/f32[8,128]{1,0:T(8,128)S(1)}) custom-call(bf16[128,384]{1,0:T(8,128)(2,1)S(1)} %bitcast.4, bf16[384,128]{1,0:T(8,128)(2,1)S(1)} %copy-done.2, f32[8,128]{1,0:T(8,128)S(1)} %stack.10.meta_ref), custom_call_target="tpu_custom_call" | custom-call | tf_op jit(solution)/shard_map/requests/pallas_call | solution.py:408
  21.3 9.0 %copy.11.pas_hbm = bf16[128,180,128]{2,1,0:T(8,128)(2,1)} copy(bf16[128,180,128]{2,0,1:T(8,128)(2,1)} %param.10) | data formatting | bytes 11796480 | tf_op args[2]
  30.4 0.0 copy-done.4
  30.4 0.0 copy-start.1
  30.4 0.0 copy-start.3
  30.4 0.0 copy-start.5
  30.4 13.9 %scores.1 = (f32[32,32,128]{2,1,0:T(8,128)S(1)}, f32[32,32,128]{2,1,0:T(8,128)S(1)}, f32[8,128]{1,0:T(8,128)S(1)}) custom-call(s32[16,128]{1,0:T(8,128)S(1)} %get-tuple-element.15.code, f32[16,128]{1,0:T(8,128)S(1)} %get-tuple-element.16.prob, f32[16,128]{1,0:T(8,128)S(1)} %get-tuple-element.17.teach, s32[128]{0:T(128)S(1)} %copy-done.4, ...), custom_call_target="tpu_custom_call" | custom-call | tf_op jit(solution)/shard_map/scores/pallas_call | solution.py:434
  44.3 0.0 copy-done.1
  44.3 0.0 copy-done.3
  44.3 0.0 copy-done.5
  44.3 49.8 %grads.1 = (f32[8,128]{1,0:T(8,128)S(1)}, bf16[128,384]{1,0:T(8,128)(2,1)S(1)}, f32[384,128]{1,0:T(8,128)S(1)}) custom-call(s32[4]{0:T(128)S(1)} %copy-done.5, f32[32,32,128]{2,1,0:T(8,128)S(1)} %get-tuple-element.19.a_ref, f32[32,32,128]{2,1,0:T(8,128)S(1)} %get-tuple-element.20.t_ref, f32[8,128]{1,0:T(8,128)S(1)} %get-tuple-element.21.stat_ref, ...), custom_call_target="tpu_custom_call" | custom-call | tf_op jit(solution)/shard_map/grads/pallas_call | solution.py:461
  94.1 0.5 slice_bitcast_fusion
  94.6 0.6 copy.14
  95.3 0.7 copy.15
  (6 shorter events, 0.0 us)
Async XLA Ops:
  4.1 0.9 copy-start
  5.0 0.9 copy-start.2
  5.9 24.5 %copy-start.4 = (s32[128]{0:T(128)S(1)}, s32[128]{0:T(128)}, u32[]{:S(2)}) copy-start(s32[128]{0:T(128)} %plen.1) | copy-start | bytes 1540
  30.4 13.9 %copy-start.1 = (bf16[4,32,384]{2,1,0:T(8,128)(2,1)S(1)}, bf16[4,32,384]{2,1,0:T(8,128)(2,1)}, u32[]{:S(2)}) copy-start(bf16[4,32,384]{2,1,0:T(8,128)(2,1)} %param.8) | copy-start | bytes 294916
  30.4 13.9 %copy-start.3 = (bf16[384,128]{1,0:T(8,128)(2,1)S(1)}, bf16[384,128]{1,0:T(8,128)(2,1)}, u32[]{:S(2)}) copy-start(bf16[384,128]{1,0:T(8,128)(2,1)} %p_ref.3) | copy-start | bytes 294916
  30.4 13.9 %copy-start.5 = (s32[4]{0:T(128)S(1)}, s32[4]{0:T(128)}, u32[]{:S(2)}) copy-start(s32[4]{0:T(128)} %qlen.1) | copy-start | bytes 52
